TPU v7x, 32 devices: a whole 2x2x4 slice. The times are simulated.
32 devices in a mesh: wa: 8 (over z, core), an: 4 (over y, x).
Axes of the slice: x: 2, y: 2, z: 4, core: 2. Of those that a mesh axis runs over, the one named last changes fastest.
Arguments:
- mass_field: float32 [64, 128, 64, 256], P(None, 'wa', 'an'), may hold values from -8 to 8
- factor_one: float32 [256, 64], replicated, may hold values from -0.375 to 0.375
- factor_two: float32 [128, 64], P('wa'), may hold values from -0.5 to 0.5
- factor_four: float32 [64, 16], replicated, may hold values from -0.75 to 0.75
Outputs:
- gram: float32 [64, 64], P('an')
All inputs are finite; a program needn't handle non-finite values.
Results may differ from a plain program's by a relative error of at most 0.0001.
Values sent between devices are 32-bit elements; how exact they have to be, the bound alone decides.
A program may use at most 128 MiB of HBM per device.

v0:
```python
import jax
import jax.numpy as jnp
from jax import lax
from jax.sharding import PartitionSpec as P


def on_device(mass_field, factor_one, factor_two, factor_four):
    highest = lax.Precision.HIGHEST
    species_count, fibre_cells, slab_cells, first_cells = mass_field.shape
    rank_one = factor_one.shape[1]
    rank_two = factor_two.shape[1]
    rank_four = factor_four.shape[1]
    reduced = jnp.dot(factor_four.T, mass_field.reshape(species_count, -1), precision=highest)
    reduced = reduced.reshape(rank_four * fibre_cells * slab_cells, first_cells)
    slab_rows = rank_one // lax.axis_size("wa")
    mixed_rows = jnp.dot(reduced, factor_one, precision=highest)
    mixed_rows = mixed_rows.reshape(rank_four, fibre_cells, slab_cells, rank_one)
    term = jnp.einsum("qjkr,jp->rkqp", mixed_rows, factor_two, precision=highest)
    summed = lax.psum(term.reshape(rank_one, slab_cells, rank_four * rank_two), "wa")
    owned_slab = lax.dynamic_slice_in_dim(summed, lax.axis_index("wa") * slab_rows, slab_rows, 0)
    partial_gram = jnp.einsum(
        "rim,rjm->ij",
        owned_slab,
        lax.all_gather(owned_slab, "an", axis=1, tiled=True),
        precision=highest,
    )
    gram_rows = lax.psum(partial_gram, "wa")
    return gram_rows / (rank_one * rank_two * rank_four)


def solution(mesh):
    in_specs = (P(None, "wa", "an", None), P(), P("wa", None), P())
    out_specs = P("an", None)
    return jax.shard_map(
        on_device, mesh=mesh, in_specs=in_specs, out_specs=out_specs, check_vma=False
    )
```

profile of v0, /device:TPU:0, one launch (start us, length us, event | category | flops | bytes accessed | tf_op | source)
XLA Modules:
  0.0 228.7 jit_solution(18144926732122515045)
XLA Ops:
  6.5 0.0 copy-start
  6.5 0.0 all-reduce.2.cloned.1.call-start
  6.5 22.7 %fusion = f32[16,16,16,256]{3,0,2,1:T(8,128)S(1)} fusion(f32[16,16,256,64]{2,1,0,3:T(8,128)} %bitcast.35, f32[64,16]{0,1:T(8,128)} %param.7), kind=kOutput, calls=%fused_computation | convolution fusion | flops 805306368 | bytes 20975616 | tf_op jit(solution)/shard_map/dot_general | solution.py:13
  29.3 0.0 copy-done
  29.3 0.0 copy-start.1
  29.3 5.6 %fusion.2 = f32[16,16,16,64]{3,1,2,0:T(8,128)S(1)} fusion(f32[16,16,16,256]{3,0,2,1:T(8,128)S(1)} %fusion, f32[256,64]{0,1:T(8,128)S(1)} %copy-done), kind=kOutput, calls=%fused_computation.2 | convolution fusion | flops 805306368 | bytes 5308416 | tf_op jit(solution)/shard_map/dot_general | solution.py:16
  34.9 0.0 copy-done.1
  34.9 13.5 %convolution_bitcast_fusion = f32[64,16,16,64]{3,0,1,2:T(8,128)S(1)} fusion(f32[16,16,16,64]{3,1,2,0:T(8,128)S(1)} %fusion.2, f32[16,64]{1,0:T(8,128)S(1)} %copy-done.1), kind=kOutput, calls=%fused_computation.4 | convolution fusion | flops 201326592 | bytes 5246976 | tf_op jit(solution)/shard_map/qjkr,jp->rkqp/dot_general | solution.py:18
  48.4 8.3 %copy.5 = f32[64,16,16,64]{3,2,1,0:T(8,128)} copy(f32[64,16,16,64]{3,0,1,2:T(8,128)S(1)} %convolution_bitcast_fusion) | data formatting | bytes 8388608 | tf_op jit(solution)/shard_map/qjkr,jp->rkqp/transpose | solution.py:18
  56.7 7.6 %reshape.12 = f32[64,16,1024]{2,1,0:T(8,128)} reshape(f32[64,16,16,64]{3,2,1,0:T(8,128)} %copy.5) | data formatting | bytes 8388608 | tf_op jit(solution)/shard_map/reshape | solution.py:19
  64.3 0.0 all-reduce.2.cloned.1.call-update
  64.4 0.0 all-gather.2.cloned.1.call-start
  64.4 99.3 %all-reduce.2.cloned.1.call-done = f32[64,16,1024]{2,1,0:T(8,128)} async-done(((f32[64,16,1024]{2,1,0:T(8,128)}), f32[64,16,1024]{2,1,0:T(8,128)}) %all-reduce.2.cloned.1.call-update) | async-done | bytes 4194320 | tf_op jit(solution)/shard_map/psum | solution.py:19
  163.7 1.9 constant_dynamic-slice_fusion
  165.6 0.0 all-gather.2.cloned.1.call-update
  165.7 35.5 %all-gather.2.cloned.1.call-done = f32[8,64,1024]{2,1,0:T(8,128)} async-done(((f32[8,16,1024]{2,1,0:T(8,128)}), f32[8,64,1024]{2,1,0:T(8,128)}) %all-gather.2.cloned.1.call-update) | async-done | bytes 2097168 | tf_op jit(solution)/shard_map/all_gather | solution.py:24
  201.2 3.5 %convolution_bitcast_fusion.1 = f32[16,64]{1,0:T(8,128)S(1)} fusion(f32[8,16,1024]{2,1,0:T(8,128)} %constant_dynamic-slice_fusion, f32[8,64,1024]{2,1,0:T(8,128)} %all-gather.2.cloned.1.call-done), kind=kOutput, calls=%fused_computation.5 | convolution fusion | flops 100663296 | bytes 2625536 | tf_op jit(solution)/shard_map/rim,rjm->ij/dot_general | solution.py:21
  204.7 16.6 %psum.15 = f32[16,64]{1,0:T(8,128)S(1)} all-reduce(f32[16,64]{1,0:T(8,128)S(1)} %convolution_bitcast_fusion.1), channel_id=1, replica_groups=mesh['wa'=8,'an'=4] {'wa'}, use_global_device_ids=true, to_apply=%region_1.0 | all-reduce | flops 1024 | bytes 8192 | tf_op jit(solution)/shard_map/psum | solution.py:27
  221.3 0.6 broadcast_multiply_fusion
Async XLA Ops:
  6.5 22.7 %copy-start = (f32[256,64]{0,1:T(8,128)S(1)}, f32[256,64]{0,1:T(8,128)}, u32[]{:S(2)}) copy-start(f32[256,64]{0,1:T(8,128)} %param.5) | copy-start | bytes 196612
  6.5 157.2 %all-reduce.2.cloned.1.call-start = ((), (), s32[]{:S(2)}) async-start(), calls=%async_computation | async-start | bytes 8388608 | tf_op jit(solution)/shard_map/psum | solution.py:19
  29.3 5.6 %copy-start.1 = (f32[16,64]{1,0:T(8,128)S(1)}, f32[16,64]{1,0:T(8,128)}, u32[]{:S(2)}) copy-start(f32[16,64]{1,0:T(8,128)} %param.6) | copy-start | bytes 12292
  64.4 136.8 %all-gather.2.cloned.1.call-start = ((), (), s32[]{:S(2)}) async-start(), calls=%async_computation.1 | async-start | bytes 2621440 | tf_op jit(solution)/shard_map/all_gather | solution.py:24
Sparse Core Ops, SparseCore 0:
  64.5 99.2 all-reduce.1
  165.8 35.3 all-gather.1
where the time goes:
time: 229 us
  waiting for transfers between devices  135 us (59%)
  matrix products  45.3 us (20%)
  local copies, waits for them, and re-layouts  17.8 us (8%)
  blocking collectives  16.6 us (7%)
  between operations  13.5 us (6%)
    psum x1, waiting for transfers between devices, on_device(): lax.psum(term.reshape(rank_one, slab_cells, rank_four * rank_two), 'wa')  99.3 us
    all_gather x1, waiting for transfers between devices, on_device(): lax.all_gather(owned_slab, 'an', axis=1, tiled=True)  35.5 us
    dot_general x1, matrix products, on_device(): jnp.dot(factor_four.T, mass_field.reshape(species_count, -1), precision=h...  22.7 us
    psum x1, blocking collectives, on_device(): gram_rows = lax.psum(partial_gram, 'wa')  16.6 us
    dot_general x1, matrix products, on_device(): jnp.einsum('qjkr,jp->rkqp', mixed_rows, factor_two, precision=highest)  13.5 us
    transpose x1, local copies, waits for them, and re-layouts, on_device(): jnp.einsum('qjkr,jp->rkqp', mixed_rows, factor_two, precision=highest)  8.34 us
    reshape x1, local copies, waits for them, and re-layouts, on_device(): term.reshape(rank_one, slab_cells, rank_four * rank_two)  7.61 us
    dot_general x1, matrix products, on_device(): mixed_rows = jnp.dot(reduced, factor_one, precision=highest)  5.6 us
  transfers between devices with their start and end apart: 2, of which 2 were waited for; matrix products, arithmetic and copies ran while one was open for 0% of the time, Pallas kernels for 0%

commit v1 on v0

v1 whole, which is shorter than its diff:
```python
import functools

import jax
import jax.numpy as jnp
from jax import lax
from jax.experimental import pallas as pl
from jax.experimental.pallas import tpu as pltpu
from jax.sharding import PartitionSpec as P

MESH = pl.DeviceIdType.MESH
F32 = jnp.float32
BF16 = jnp.bfloat16
LANES = 128
SUB = 8


def iota(shape, dim):
    return lax.broadcasted_iota(jnp.int32, shape, dim)


def split(x):
    hi = x.astype(BF16)
    return hi, (x - hi.astype(F32)).astype(BF16)


def dot(a, b):
    return jnp.dot(a, b, preferred_element_type=F32)


def dot_nt(a, b):
    return lax.dot_general(a, b, (((1,), (1,)), ((), ())), preferred_element_type=F32)


def one_hot(shape, row, column):
    return jnp.where(row(iota(shape, 0)) == column(iota(shape, 1)), 1.0, 0.0).astype(BF16)


def near_first(count):
    half = count // 2
    return sorted(range(1, count), key=lambda o: (abs(o - half), o))


def kernel(
    nw, na, chunks, group,
    x_hbm, f1t_ref, f2_ref, f4t_ref, out_ref,
    xbuf, a1, f1s, red, f2all, a2, mix, got, proj, rows, part, part_in, term, term_in,
    x_sem, f2_send, f2_recv, mix_send, mix_recv, row_send, row_recv, part_send, part_recv, term_send, term_recv,
):
    me = lax.axis_index("wa")
    mine = lax.axis_index("an")
    species, fibre, slab, first = x_hbm.shape
    rank_one = f1t_ref.shape[0]
    rank_two = f2_ref.shape[1]
    rank_four = f4t_ref.shape[0]
    width = mix.shape[-1]
    q_groups = rank_four * slab // width
    per = fibre // chunks
    all_fibre = nw * fibre
    kept = rank_two * SUB
    share = kept // na
    wa_offsets = near_first(nw)
    an_offsets = near_first(na)

    def wa_peer(o):
        return lax.rem(me + o, nw)

    def an_peer(o):
        return lax.rem(mine + o, na)

    def load(j):
        return pltpu.make_async_copy(x_hbm.at[:, j], xbuf.at[j], x_sem.at[j])

    def start_load(j, carry):
        load(j).start()
        return carry

    lax.fori_loop(0, fibre, start_load, 0)

    barrier = pltpu.get_barrier_semaphore()
    for o in wa_offsets:
        pl.semaphore_signal(barrier, inc=1, device_id=(wa_peer(o), mine), device_id_type=MESH)
    for o in an_offsets:
        pl.semaphore_signal(barrier, inc=1, device_id=(me, an_peer(o)), device_id_type=MESH)

    f4hi, f4lo = split(f4t_ref[...])
    n1 = rank_four * SUB
    spread = one_hot((n1, rank_four), lambda r: r >> 3, lambda c: c)
    widen = one_hot((species, species * SUB), lambda r: r, lambda c: c >> 3)
    same = (iota((n1, species * SUB), 0) & 7) == (iota((n1, species * SUB), 1) & 7)
    for half, part4 in enumerate((f4hi, f4lo)):
        full = dot(dot(spread, part4).astype(BF16), widen)
        a1[half * n1 : (half + 1) * n1, :] = jnp.where(same, full, 0.0).astype(BF16)
    f1hi, f1lo = split(f1t_ref[...])
    f1s[:rank_one, :] = f1hi
    f1s[rank_one:, :] = f1lo
    f2all[me] = f2_ref[...]

    pl.semaphore_wait(barrier, nw + na - 2)

    def f2_copy(o):
        return pltpu.make_async_remote_copy(
            src_ref=f2all.at[me], dst_ref=f2all.at[me],
            send_sem=f2_send.at[o], recv_sem=f2_recv.at[o],
            device_id=(wa_peer(o), mine), device_id_type=MESH,
        )

    for o in wa_offsets:
        f2_copy(o).start()

    def mix_copy(c, o):
        peer = wa_peer(o)
        return pltpu.make_async_remote_copy(
            src_ref=mix.at[c, peer], dst_ref=got.at[c, me],
            send_sem=mix_send.at[c, o], recv_sem=mix_recv.at[c, o],
            device_id=(peer, mine), device_id_type=MESH,
        )

    def one_fibre(j, c, jj):
        for kh in range(slab // SUB):
            block = xbuf[j, :, kh * SUB : (kh + 1) * SUB, :].reshape(species * SUB, first)
            hi, lo = split(block)
            both = dot(a1[...], hi)
            reduced = both[:n1] + both[n1:] + dot(a1[:n1, :], lo)
            red[jj, :, kh * SUB : (kh + 1) * SUB, :] = reduced.reshape(rank_four, SUB, first)
        hi, lo = split(red[jj].reshape(rank_four * slab, first))
        both = dot_nt(f1s[...], hi)
        mixed = both[:rank_one] + both[rank_one:] + dot_nt(f1s[:rank_one, :], lo)
        for d in range(nw):
            rg, qg = d // q_groups, d % q_groups
            mix[c, d, jj] = mixed[rg * SUB : (rg + 1) * SUB, qg * width : (qg + 1) * width]

    def produce(c, carry):
        for jj in range(per):
            load(c * per + jj).wait()
            one_fibre(c * per + jj, c, jj)
        for o in wa_offsets:
            mix_copy(c, o).start()
        got[c, me] = mix[c, me]
        return carry

    lax.fori_loop(0, chunks, produce, 0)

    for o in wa_offsets:
        f2_copy(o).wait()
    f2hi, f2lo = split(f2all[...].reshape(all_fibre, rank_two))
    spread2 = one_hot((kept, rank_two), lambda r: r >> 3, lambda c: c)
    depth = nw * per * SUB
    same2 = (iota((kept, depth), 0) & 7) == (iota((kept, depth), 1) & 7)
    rows_hi = dot_nt(spread2, f2hi).astype(BF16)
    rows_lo = dot_nt(spread2, f2lo).astype(BF16)

    def expand(c, carry):
        def fibre_of(col):
            unit = col >> 3
            return (unit // per) * fibre + c * per + unit % per

        pick = one_hot((all_fibre, depth), lambda r: r, fibre_of)
        a2[c, :kept, :] = jnp.where(same2, dot(rows_hi, pick), 0.0).astype(BF16)
        a2[c, kept:, :] = jnp.where(same2, dot(rows_lo, pick), 0.0).astype(BF16)
        return carry

    lax.fori_loop(0, chunks, expand, 0)
    proj[...] = jnp.zeros_like(proj)

    def project(c, carry):
        for o in wa_offsets:
            mix_copy(c, o).wait()
        hi, lo = split(got[c].reshape(depth, width))
        both = dot(a2[c], hi)
        proj[...] += both[:kept] + both[kept:] + dot(a2[c, :kept, :], lo)
        return carry

    lax.fori_loop(0, chunks, project, 0)

    def row_copy(o):
        peer = an_peer(o)
        return pltpu.make_async_remote_copy(
            src_ref=proj.at[pl.ds(pl.multiple_of(peer * share, SUB), share)], dst_ref=rows.at[mine],
            send_sem=row_send.at[o], recv_sem=row_recv.at[o],
            device_id=(me, peer), device_id_type=MESH,
        )

    for o in an_offsets:
        row_copy(o).start()
    rows[mine] = proj[pl.ds(pl.multiple_of(mine * share, SUB), share), :]
    for o in an_offsets:
        row_copy(o).wait()

    halves = width // LANES
    stack = jnp.concatenate(
        [
            jnp.concatenate([rows[a, :, h * LANES : (h + 1) * LANES] for a in range(na)], axis=1)
            for h in range(halves)
        ],
        axis=0,
    )
    hi, lo = split(stack)
    thi, tlo = split(stack.T)
    q_row = iota((LANES, LANES), 0) // slab
    q_col = iota((LANES, LANES), 1) // slab
    lane_block = iota((na * slab, LANES), 1) // slab
    total = jnp.zeros((na * slab, LANES), F32)
    for b in range(na):
        at = slice(b * LANES, (b + 1) * LANES)
        wide = dot(thi, hi[:, at]) + dot(thi, lo[:, at]) + dot(tlo, hi[:, at])
        wide = wide.reshape(na, LANES, LANES)
        wide = jnp.where((q_row == q_col)[None], wide, 0.0)
        wide = wide.reshape(na, LANES // slab, slab, LANES).sum(axis=1).reshape(na * slab, LANES)
        shift = LANES // 2
        while shift >= slab:
            wide = wide + pltpu.roll(wide, shift, 1)
            shift //= 2
        total = jnp.where(lane_block == b, wide, total)
    part[...] = total.reshape(na, slab, LANES)

    def part_copy(o):
        peer = an_peer(o)
        return pltpu.make_async_remote_copy(
            src_ref=part.at[peer], dst_ref=part_in.at[mine],
            send_sem=part_send.at[o], recv_sem=part_recv.at[o],
            device_id=(me, peer), device_id_type=MESH,
        )

    for o in an_offsets:
        part_copy(o).start()
    part_in[mine] = part[mine]
    for o in an_offsets:
        part_copy(o).wait()
    term[...] = part_in[...].sum(axis=0)

    def term_copy(o):
        return pltpu.make_async_remote_copy(
            src_ref=term, dst_ref=term_in.at[me],
            send_sem=term_send.at[o], recv_sem=term_recv.at[o],
            device_id=(wa_peer(o), mine), device_id_type=MESH,
        )

    for o in wa_offsets:
        term_copy(o).start()
    term_in[me] = term[...]
    for o in wa_offsets:
        term_copy(o).wait()
    out_ref[...] = term_in[...].sum(axis=0)


def on_device(mass_field, factor_one, factor_two, factor_four):
    nw, na = lax.axis_size("wa"), lax.axis_size("an")
    species, fibre, slab, first = mass_field.shape
    rank_one, rank_two, rank_four = factor_one.shape[1], factor_two.shape[1], factor_four.shape[1]
    chunks = 4
    per = fibre // chunks
    width = rank_one * rank_four * slab // (nw * SUB)
    kept = rank_two * SUB
    share = kept // na
    depth = nw * per * SUB
    dma = pltpu.SemaphoreType.DMA
    vmem = pl.BlockSpec(memory_space=pltpu.VMEM)
    summed = pl.pallas_call(
        functools.partial(kernel, nw, na, chunks, SUB),
        out_shape=jax.ShapeDtypeStruct((slab, LANES), F32),
        in_specs=[pl.BlockSpec(memory_space=pl.ANY), vmem, vmem, vmem],
        out_specs=vmem,
        scratch_shapes=[
            pltpu.VMEM((fibre, species, slab, first), F32),
            pltpu.VMEM((2 * rank_four * SUB, species * SUB), BF16),
            pltpu.VMEM((2 * rank_one, first), BF16),
            pltpu.VMEM((per, rank_four, slab, first), F32),
            pltpu.VMEM((nw, fibre, rank_two), F32),
            pltpu.VMEM((chunks, 2 * kept, depth), BF16),
            pltpu.VMEM((chunks, nw, per, SUB, width), F32),
            pltpu.VMEM((chunks, nw, per, SUB, width), F32),
            pltpu.VMEM((kept, width), F32),
            pltpu.VMEM((na, share, width), F32),
            pltpu.VMEM((na, slab, LANES), F32),
            pltpu.VMEM((na, slab, LANES), F32),
            pltpu.VMEM((slab, LANES), F32),
            pltpu.VMEM((nw, slab, LANES), F32),
            dma((fibre,)),
            dma((nw,)), dma((nw,)),
            dma((chunks, nw)), dma((chunks, nw)),
            dma((na,)), dma((na,)),
            dma((na,)), dma((na,)),
            dma((nw,)), dma((nw,)),
        ],
        compiler_params=pltpu.CompilerParams(
            collective_id=0, has_side_effects=True, vmem_limit_bytes=48 * 1024 * 1024
        ),
    )(mass_field, factor_one.T, factor_two, factor_four.T)
    return summed[:, : na * slab] / (rank_one * rank_two * rank_four)


def solution(mesh):
    in_specs = (P(None, "wa", "an", None), P(), P("wa", None), P())
    out_specs = P("an", None)
    return jax.shard_map(
        on_device, mesh=mesh, in_specs=in_specs, out_specs=out_specs, check_vma=False
    )
```

time: 229 us -> 51.6 us (0.23)
  waiting for transfers between devices: 135 us -> 0 us
  Pallas kernels: 0 us -> 48.5 us
  matrix products: 45.3 us -> 0 us
  blocking collectives: 16.6 us -> 0 us
  local copies, waits for them, and re-layouts: 17.8 us -> 2.23 us
  between operations: 13.5 us -> 0.01 us
    psum x1 -> x0, waiting for transfers between devices: 99.3 us -> none  [on_device(): lax.psum(term.reshape(rank_one, slab_cells, rank_four * rank_two), 'wa')]
    pallas_call x0 -> x1, Pallas kernels: none -> 48.5 us  [on_device(): pl.pallas_call(functools.partial(kernel, nw, na, chunks, SUB), out_shape=...]
    dot_general x4 -> x0, matrix products: 45.3 us -> none  [the longest x1 22.7 us: on_device(): jnp.dot(factor_four.T, mass_field.reshape(species_count, -1), precision=h...]
    all_gather x1 -> x0, waiting for transfers between devices: 35.5 us -> none  [on_device(): lax.all_gather(owned_slab, 'an', axis=1, tiled=True)]
    psum x1 -> x0, blocking collectives: 16.6 us -> none  [on_device(): gram_rows = lax.psum(partial_gram, 'wa')]
    transpose x1 -> x0, local copies, waits for them, and re-layouts: 8.34 us -> none  [on_device(): jnp.einsum('qjkr,jp->rkqp', mixed_rows, factor_two, precision=highest)]
    reshape x1 -> x0, local copies, waits for them, and re-layouts: 7.61 us -> none  [on_device(): term.reshape(rank_one, slab_cells, rank_four * rank_two)]
  transfers between devices with their start and end apart: 2 -> 0, of which waited for: 2 -> 0; matrix products, arithmetic and copies ran while one was open for 0% -> 0% of each run, Pallas kernels for 0% -> 0%
where the time goes in v1:
time: 51.6 us; the launch traced here: 51.4 us
  Pallas kernels  48.5 us (94%)
  local copies, waits for them, and re-layouts  2.23 us (4%)
  other arithmetic  0.6 us (1%)
    pallas_call x1, Pallas kernels, on_device(): pl.pallas_call(functools.partial(kernel, nw, na, chunks, SUB), out_shape=...  48.5 us
    unnamed x6, local copies, waits for them, and re-layouts  2.23 us

profile of v1, /device:TPU:0, one launch (start us, length us, event | category | flops | bytes accessed | tf_op | source)
XLA Modules:
  0.0 51.4 jit_solution(9412926613567409665)
XLA Ops:
  0.0 0.0 copy-start
  0.0 0.8 %copy-done = f32[256,64]{0,1:T(8,128)S(1)} copy-done((f32[256,64]{0,1:T(8,128)S(1)}, f32[256,64]{0,1:T(8,128)}, u32[]{:S(2)}) %copy-start) | copy-done | bytes 65560
  0.8 0.0 copy-start.1
  0.8 0.7 %copy-done.1 = f32[16,64]{1,0:T(8,128)S(1)} copy-done((f32[16,64]{1,0:T(8,128)S(1)}, f32[16,64]{1,0:T(8,128)}, u32[]{:S(2)}) %copy-start.1) | copy-done | bytes 4120
  1.5 0.0 copy-start.2
  1.5 0.7 %copy-done.2 = f32[64,16]{0,1:T(8,128)S(1)} copy-done((f32[64,16]{0,1:T(8,128)S(1)}, f32[64,16]{0,1:T(8,128)}, u32[]{:S(2)}) %copy-start.2) | copy-done | bytes 4120
  2.2 48.5 %shard_map.46 = f32[16,128]{1,0:T(8,128)S(1)} custom-call(f32[64,16,16,256]{3,2,1,0:T(8,128)} %x_hbm.1, f32[64,256]{1,0:T(8,128)S(1)} %bitcast.2, f32[16,64]{1,0:T(8,128)S(1)} %copy-done.1, f32[16,64]{1,0:T(8,128)S(1)} %bitcast.3), custom_call_target="tpu_custom_call" | custom-call | tf_op jit(solution)/shard_map/pallas_call | solution.py:258
  50.8 0.6 %slice_multiply_fusion = f32[16,64]{1,0:T(8,128)} fusion(f32[16,128]{1,0:T(8,128)S(1)} %shard_map.46), kind=kLoop, calls=%fused_computation | loop fusion | flops 1024 | bytes 8192 | tf_op jit(solution)/shard_map/div | solution.py:289
Async XLA Ops:
  0.0 0.8 %copy-start = (f32[256,64]{0,1:T(8,128)S(1)}, f32[256,64]{0,1:T(8,128)}, u32[]{:S(2)}) copy-start(f32[256,64]{0,1:T(8,128)} %param.5) | copy-start | bytes 196612
  0.8 0.7 %copy-start.1 = (f32[16,64]{1,0:T(8,128)S(1)}, f32[16,64]{1,0:T(8,128)}, u32[]{:S(2)}) copy-start(f32[16,64]{1,0:T(8,128)} %f2_ref.1) | copy-start | bytes 12292
  1.5 0.7 %copy-start.2 = (f32[64,16]{0,1:T(8,128)S(1)}, f32[64,16]{0,1:T(8,128)}, u32[]{:S(2)}) copy-start(f32[64,16]{0,1:T(8,128)} %param.7) | copy-start | bytes 12292

commit v2 on v1

--- a/solution.py
+++ b/solution.py
@@ -41,9 +41,9 @@
 
 
 def kernel(
-    nw, na, chunks, group,
-    x_hbm, f1t_ref, f2_ref, f4t_ref, out_ref,
-    xbuf, a1, f1s, red, f2all, a2, mix, got, proj, rows, part, part_in, term, term_in,
+    nw, na, chunks,
+    x_hbm, f1t_hbm, f2_hbm, f4t_hbm, out_ref,
+    f1t_ref, f2_ref, f4t_ref, small_sem, xbuf, a1, f1s, red, f2all, a2, mix, got, proj, rows, part, part_in, term, term_in,
     x_sem, f2_send, f2_recv, mix_send, mix_recv, row_send, row_recv, part_send, part_recv, term_send, term_recv,
 ):
     me = lax.axis_index("wa")
@@ -52,7 +52,8 @@
     rank_one = f1t_ref.shape[0]
     rank_two = f2_ref.shape[1]
     rank_four = f4t_ref.shape[0]
-    width = mix.shape[-1]
+    halves = mix.shape[1]
+    width = halves * LANES
     q_groups = rank_four * slab // width
     per = fibre // chunks
     all_fibre = nw * fibre
@@ -67,6 +68,13 @@
     def an_peer(o):
         return lax.rem(mine + o, na)
 
+    small = [
+        pltpu.make_async_copy(src, dst, small_sem.at[n])
+        for n, (src, dst) in enumerate(((f4t_hbm, f4t_ref), (f1t_hbm, f1t_ref), (f2_hbm, f2_ref)))
+    ]
+    for copy in small:
+        copy.start()
+
     def load(j):
         return pltpu.make_async_copy(x_hbm.at[:, j], xbuf.at[j], x_sem.at[j])
 
@@ -82,6 +90,8 @@
     for o in an_offsets:
         pl.semaphore_signal(barrier, inc=1, device_id=(me, an_peer(o)), device_id_type=MESH)
 
+    for copy in small:
+        copy.wait()
     f4hi, f4lo = split(f4t_ref[...])
     n1 = rank_four * SUB
     spread = one_hot((n1, rank_four), lambda r: r >> 3, lambda c: c)
@@ -107,11 +117,11 @@
     for o in wa_offsets:
         f2_copy(o).start()
 
-    def mix_copy(c, o):
+    def mix_copy(c, h, o):
         peer = wa_peer(o)
         return pltpu.make_async_remote_copy(
-            src_ref=mix.at[c, peer], dst_ref=got.at[c, me],
-            send_sem=mix_send.at[c, o], recv_sem=mix_recv.at[c, o],
+            src_ref=mix.at[c, h, peer], dst_ref=got.at[c, h, me],
+            send_sem=mix_send.at[c, h, o], recv_sem=mix_recv.at[c, h, o],
             device_id=(peer, mine), device_id_type=MESH,
         )
 
@@ -127,18 +137,31 @@
         mixed = both[:rank_one] + both[rank_one:] + dot_nt(f1s[:rank_one, :], lo)
         for d in range(nw):
             rg, qg = d // q_groups, d % q_groups
-            mix[c, d, jj] = mixed[rg * SUB : (rg + 1) * SUB, qg * width : (qg + 1) * width]
+            for h in range(halves):
+                lane = qg * width + h * LANES
+                mix[c, h, d, jj] = mixed[rg * SUB : (rg + 1) * SUB, lane : lane + LANES]
 
     def produce(c, carry):
         for jj in range(per):
             load(c * per + jj).wait()
             one_fibre(c * per + jj, c, jj)
+        send(c, 0)
+        for h in range(halves):
+            got[c, h, me] = mix[c, h, me]
+        return carry
+
+    def send(c, h):
         for o in wa_offsets:
-            mix_copy(c, o).start()
-        got[c, me] = mix[c, me]
+            mix_copy(c, h, o).start()
+
+    def send_later(c, carry):
+        for h in range(1, halves):
+            send(c, h)
         return carry
 
     lax.fori_loop(0, chunks, produce, 0)
+    if halves > 1:
+        lax.fori_loop(0, chunks, send_later, 0)
 
     for o in wa_offsets:
         f2_copy(o).wait()
@@ -162,55 +185,57 @@
     lax.fori_loop(0, chunks, expand, 0)
     proj[...] = jnp.zeros_like(proj)
 
-    def project(c, carry):
-        for o in wa_offsets:
-            mix_copy(c, o).wait()
-        hi, lo = split(got[c].reshape(depth, width))
-        both = dot(a2[c], hi)
-        proj[...] += both[:kept] + both[kept:] + dot(a2[c, :kept, :], lo)
-        return carry
-
-    lax.fori_loop(0, chunks, project, 0)
-
-    def row_copy(o):
+    def project(h):
+        def add(c, carry):
+            for o in wa_offsets:
+                mix_copy(c, h, o).wait()
+            hi, lo = split(got[c, h].reshape(depth, LANES))
+            both = dot(a2[c], hi)
+            proj[h] += both[:kept] + both[kept:] + dot(a2[c, :kept, :], lo)
+            return carry
+
+        lax.fori_loop(0, chunks, add, 0)
+
+    def row_copy(h, o):
         peer = an_peer(o)
         return pltpu.make_async_remote_copy(
-            src_ref=proj.at[pl.ds(pl.multiple_of(peer * share, SUB), share)], dst_ref=rows.at[mine],
-            send_sem=row_send.at[o], recv_sem=row_recv.at[o],
+            src_ref=proj.at[h, pl.ds(pl.multiple_of(peer * share, SUB), share)], dst_ref=rows.at[h, mine],
+            send_sem=row_send.at[h, o], recv_sem=row_recv.at[h, o],
             device_id=(me, peer), device_id_type=MESH,
         )
 
-    for o in an_offsets:
-        row_copy(o).start()
-    rows[mine] = proj[pl.ds(pl.multiple_of(mine * share, SUB), share), :]
-    for o in an_offsets:
-        row_copy(o).wait()
-
-    halves = width // LANES
-    stack = jnp.concatenate(
-        [
-            jnp.concatenate([rows[a, :, h * LANES : (h + 1) * LANES] for a in range(na)], axis=1)
-            for h in range(halves)
-        ],
-        axis=0,
-    )
-    hi, lo = split(stack)
-    thi, tlo = split(stack.T)
     q_row = iota((LANES, LANES), 0) // slab
     q_col = iota((LANES, LANES), 1) // slab
     lane_block = iota((na * slab, LANES), 1) // slab
-    total = jnp.zeros((na * slab, LANES), F32)
-    for b in range(na):
-        at = slice(b * LANES, (b + 1) * LANES)
-        wide = dot(thi, hi[:, at]) + dot(thi, lo[:, at]) + dot(tlo, hi[:, at])
-        wide = wide.reshape(na, LANES, LANES)
-        wide = jnp.where((q_row == q_col)[None], wide, 0.0)
-        wide = wide.reshape(na, LANES // slab, slab, LANES).sum(axis=1).reshape(na * slab, LANES)
-        shift = LANES // 2
-        while shift >= slab:
-            wide = wide + pltpu.roll(wide, shift, 1)
-            shift //= 2
-        total = jnp.where(lane_block == b, wide, total)
+
+    def gram_of(h):
+        stack = jnp.concatenate([rows[h, a] for a in range(na)], axis=1)
+        hi, lo = split(stack)
+        thi, tlo = split(stack.T)
+        total = jnp.zeros((na * slab, LANES), F32)
+        for b in range(na):
+            at = slice(b * LANES, (b + 1) * LANES)
+            wide = dot(thi, hi[:, at]) + dot(thi, lo[:, at]) + dot(tlo, hi[:, at])
+            wide = wide.reshape(na, LANES, LANES)
+            wide = jnp.where((q_row == q_col)[None], wide, 0.0)
+            wide = wide.reshape(na, LANES // slab, slab, LANES).sum(axis=1).reshape(na * slab, LANES)
+            shift = LANES // 2
+            while shift >= slab:
+                wide = wide + pltpu.roll(wide, shift, 1)
+                shift //= 2
+            total = jnp.where(lane_block == b, wide, total)
+        return total
+
+    total = None
+    for h in range(halves):
+        project(h)
+        for o in an_offsets:
+            row_copy(h, o).start()
+        rows[h, mine] = proj[h, pl.ds(pl.multiple_of(mine * share, SUB), share), :]
+        for o in an_offsets:
+            row_copy(h, o).wait()
+        gram_half = gram_of(h)
+        total = gram_half if total is None else total + gram_half
     part[...] = total.reshape(na, slab, LANES)
 
     def part_copy(o):
@@ -249,41 +274,45 @@
     rank_one, rank_two, rank_four = factor_one.shape[1], factor_two.shape[1], factor_four.shape[1]
     chunks = 4
     per = fibre // chunks
-    width = rank_one * rank_four * slab // (nw * SUB)
+    halves = rank_one * rank_four * slab // (nw * SUB * LANES)
     kept = rank_two * SUB
     share = kept // na
     depth = nw * per * SUB
     dma = pltpu.SemaphoreType.DMA
     vmem = pl.BlockSpec(memory_space=pltpu.VMEM)
     summed = pl.pallas_call(
-        functools.partial(kernel, nw, na, chunks, SUB),
+        functools.partial(kernel, nw, na, chunks),
         out_shape=jax.ShapeDtypeStruct((slab, LANES), F32),
-        in_specs=[pl.BlockSpec(memory_space=pl.ANY), vmem, vmem, vmem],
+        in_specs=[pl.BlockSpec(memory_space=pl.ANY)] * 4,
         out_specs=vmem,
         scratch_shapes=[
+            pltpu.VMEM((rank_one, first), F32),
+            pltpu.VMEM((fibre, rank_two), F32),
+            pltpu.VMEM((rank_four, species), F32),
+            dma((3,)),
             pltpu.VMEM((fibre, species, slab, first), F32),
             pltpu.VMEM((2 * rank_four * SUB, species * SUB), BF16),
             pltpu.VMEM((2 * rank_one, first), BF16),
             pltpu.VMEM((per, rank_four, slab, first), F32),
             pltpu.VMEM((nw, fibre, rank_two), F32),
             pltpu.VMEM((chunks, 2 * kept, depth), BF16),
-            pltpu.VMEM((chunks, nw, per, SUB, width), F32),
-            pltpu.VMEM((chunks, nw, per, SUB, width), F32),
-            pltpu.VMEM((kept, width), F32),
-            pltpu.VMEM((na, share, width), F32),
+            pltpu.VMEM((chunks, halves, nw, per, SUB, LANES), F32),
+            pltpu.VMEM((chunks, halves, nw, per, SUB, LANES), F32),
+            pltpu.VMEM((halves, kept, LANES), F32),
+            pltpu.VMEM((halves, na, share, LANES), F32),
             pltpu.VMEM((na, slab, LANES), F32),
             pltpu.VMEM((na, slab, LANES), F32),
             pltpu.VMEM((slab, LANES), F32),
             pltpu.VMEM((nw, slab, LANES), F32),
             dma((fibre,)),
             dma((nw,)), dma((nw,)),
-            dma((chunks, nw)), dma((chunks, nw)),
-            dma((na,)), dma((na,)),
+            dma((chunks, halves, nw)), dma((chunks, halves, nw)),
+            dma((halves, na)), dma((halves, na)),
             dma((na,)), dma((na,)),
             dma((nw,)), dma((nw,)),
         ],
         compiler_params=pltpu.CompilerParams(
-            collective_id=0, has_side_effects=True, vmem_limit_bytes=48 * 1024 * 1024
+            collective_id=0, has_side_effects=True, vmem_limit_bytes=56 * 1024 * 1024
         ),
     )(mass_field, factor_one.T, factor_two, factor_four.T)
     return summed[:, : na * slab] / (rank_one * rank_two * rank_four)

time: 51.6 us -> 49.2 us (0.953)
  local copies, waits for them, and re-layouts: 2.23 us -> 0 us
  Pallas kernels: 48.5 us -> 47.6 us
  other arithmetic: 0.6 us -> 1.3 us
    unnamed x6 -> x0, local copies, waits for them, and re-layouts: 2.23 us -> none
    pallas_call x1, Pallas kernels: 48.5 us -> 47.6 us  [on_device(): pl.pallas_call(functools.partial(kernel, nw, na, chunks), out_shape=jax.S...]
    div x1, other arithmetic: 0.6 us -> 1.3 us  [on_device(): return summed[:, :na * slab] / (rank_one * rank_two * rank_four)]
where the time goes in v2:
time: 49.2 us; the launch traced here: 48.9 us
  Pallas kernels  47.6 us (97%)
  other arithmetic  1.3 us (3%)
    pallas_call x1, Pallas kernels, on_device(): pl.pallas_call(functools.partial(kernel, nw, na, chunks), out_shape=jax.S...  47.6 us
    div x1, other arithmetic, on_device(): return summed[:, :na * slab] / (rank_one * rank_two * rank_four)  1.3 us

profile of v2, /device:TPU:0, one launch (start us, length us, event | category | flops | bytes accessed | tf_op | source)
XLA Modules:
  0.0 48.9 jit_solution(17819777548251971218)
XLA Ops:
  0.0 47.6 %shard_map.46 = f32[16,128]{1,0:T(8,128)} custom-call(f32[64,16,16,256]{3,2,1,0:T(8,128)} %x_hbm.1, f32[64,256]{1,0:T(8,128)} %bitcast.2, f32[16,64]{1,0:T(8,128)} %f2_hbm.1, f32[16,64]{1,0:T(8,128)} %bitcast.3), custom_call_target="tpu_custom_call" | custom-call | tf_op jit(solution)/shard_map/pallas_call | solution.py:283
  47.6 1.3 %slice_multiply_fusion = f32[16,64]{1,0:T(8,128)} fusion(f32[16,128]{1,0:T(8,128)} %shard_map.46), kind=kLoop, calls=%fused_computation | loop fusion | flops 1024 | bytes 8192 | tf_op jit(solution)/shard_map/div | solution.py:318

commit v3 on v2

--- a/solution.py
+++ b/solution.py
@@ -125,13 +125,15 @@
             device_id=(peer, mine), device_id_type=MESH,
         )
 
-    def one_fibre(j, c, jj):
+    def reduce_species(j, jj):
         for kh in range(slab // SUB):
             block = xbuf[j, :, kh * SUB : (kh + 1) * SUB, :].reshape(species * SUB, first)
             hi, lo = split(block)
             both = dot(a1[...], hi)
             reduced = both[:n1] + both[n1:] + dot(a1[:n1, :], lo)
             red[jj, :, kh * SUB : (kh + 1) * SUB, :] = reduced.reshape(rank_four, SUB, first)
+
+    def mix_first(c, jj):
         hi, lo = split(red[jj].reshape(rank_four * slab, first))
         both = dot_nt(f1s[...], hi)
         mixed = both[:rank_one] + both[rank_one:] + dot_nt(f1s[:rank_one, :], lo)
@@ -144,7 +146,10 @@
     def produce(c, carry):
         for jj in range(per):
             load(c * per + jj).wait()
-            one_fibre(c * per + jj, c, jj)
+        for jj in range(per):
+            reduce_species(c * per + jj, jj)
+        for jj in range(per):
+            mix_first(c, jj)
         send(c, 0)
         for h in range(halves):
             got[c, h, me] = mix[c, h, me]
@@ -154,14 +159,21 @@
         for o in wa_offsets:
             mix_copy(c, h, o).start()
 
-    def send_later(c, carry):
+    def send_rest(c):
         for h in range(1, halves):
             send(c, h)
+
+    lag = chunks // 2
+    lax.fori_loop(0, lag, produce, 0)
+
+    def produce_and_send(c, carry):
+        produce(c, carry)
+        send_rest(c - lag)
         return carry
 
-    lax.fori_loop(0, chunks, produce, 0)
-    if halves > 1:
-        lax.fori_loop(0, chunks, send_later, 0)
+    lax.fori_loop(lag, chunks, produce_and_send, 0)
+    for c in range(chunks - lag, chunks):
+        send_rest(c)
 
     for o in wa_offsets:
         f2_copy(o).wait()

time: 49.2 us -> 51.8 us (1.053)
  Pallas kernels: 47.6 us -> 50.3 us
    pallas_call x1, Pallas kernels: 47.6 us -> 50.3 us  [on_device(): pl.pallas_call(functools.partial(kernel, nw, na, chunks), out_shape=jax.S...]
where the time goes in v3:
time: 51.8 us; the launch traced here: 51.6 us
  Pallas kernels  50.3 us (97%)
  other arithmetic  1.3 us (3%)
    pallas_call x1, Pallas kernels, on_device(): pl.pallas_call(functools.partial(kernel, nw, na, chunks), out_shape=jax.S...  50.3 us
    div x1, other arithmetic, on_device(): return summed[:, :na * slab] / (rank_one * rank_two * rank_four)  1.3 us

profile of v3, /device:TPU:0, one launch (start us, length us, event | category | flops | bytes accessed | tf_op | source)
XLA Modules:
  0.0 51.6 jit_solution(2464163511743635371)
XLA Ops:
  0.0 50.3 %shard_map.46 = f32[16,128]{1,0:T(8,128)} custom-call(f32[64,16,16,256]{3,2,1,0:T(8,128)} %x_hbm.1, f32[64,256]{1,0:T(8,128)} %bitcast.2, f32[16,64]{1,0:T(8,128)} %f2_hbm.1, f32[16,64]{1,0:T(8,128)} %bitcast.3), custom_call_target="tpu_custom_call" | custom-call | tf_op jit(solution)/shard_map/pallas_call | solution.py:295
  50.3 1.3 %slice_multiply_fusion = f32[16,64]{1,0:T(8,128)} fusion(f32[16,128]{1,0:T(8,128)} %shard_map.46), kind=kLoop, calls=%fused_computation | loop fusion | flops 1024 | bytes 8192 | tf_op jit(solution)/shard_map/div | solution.py:330

commit v4 on v2

--- a/solution.py
+++ b/solution.py
@@ -52,7 +52,7 @@
     rank_one = f1t_ref.shape[0]
     rank_two = f2_ref.shape[1]
     rank_four = f4t_ref.shape[0]
-    halves = mix.shape[1]
+    halves = mix.shape[0]
     width = halves * LANES
     q_groups = rank_four * slab // width
     per = fibre // chunks
@@ -105,8 +105,6 @@
     f1s[rank_one:, :] = f1lo
     f2all[me] = f2_ref[...]
 
-    pl.semaphore_wait(barrier, nw + na - 2)
-
     def f2_copy(o):
         return pltpu.make_async_remote_copy(
             src_ref=f2all.at[me], dst_ref=f2all.at[me],
@@ -114,13 +112,11 @@
             device_id=(wa_peer(o), mine), device_id_type=MESH,
         )
 
-    for o in wa_offsets:
-        f2_copy(o).start()
-
     def mix_copy(c, h, o):
         peer = wa_peer(o)
-        return pltpu.make_async_remote_copy(
-            src_ref=mix.at[c, h, peer], dst_ref=got.at[c, h, me],
+        span = pl.ds(c, 1 if h == 0 else 2)
+        return pltpu.make_async_remote_copy(
+            src_ref=mix.at[h, peer, span], dst_ref=got.at[h, me, span],
             send_sem=mix_send.at[c, h, o], recv_sem=mix_recv.at[c, h, o],
             device_id=(peer, mine), device_id_type=MESH,
         )
@@ -139,29 +135,33 @@
             rg, qg = d // q_groups, d % q_groups
             for h in range(halves):
                 lane = qg * width + h * LANES
-                mix[c, h, d, jj] = mixed[rg * SUB : (rg + 1) * SUB, lane : lane + LANES]
-
-    def produce(c, carry):
+                mix[h, d, c, jj] = mixed[rg * SUB : (rg + 1) * SUB, lane : lane + LANES]
+
+    def compute(c):
         for jj in range(per):
             load(c * per + jj).wait()
             one_fibre(c * per + jj, c, jj)
+        for h in range(halves):
+            got[h, me, c] = mix[h, me, c]
+
+    def produce(c, carry):
+        compute(c)
         send(c, 0)
-        for h in range(halves):
-            got[c, h, me] = mix[c, h, me]
         return carry
 
     def send(c, h):
         for o in wa_offsets:
             mix_copy(c, h, o).start()
 
-    def send_later(c, carry):
-        for h in range(1, halves):
+    compute(0)
+    pl.semaphore_wait(barrier, nw + na - 2)
+    send(0, 0)
+    for o in wa_offsets:
+        f2_copy(o).start()
+    lax.fori_loop(1, chunks, produce, 0)
+    for h in range(1, halves):
+        for c in range(0, chunks, 2):
             send(c, h)
-        return carry
-
-    lax.fori_loop(0, chunks, produce, 0)
-    if halves > 1:
-        lax.fori_loop(0, chunks, send_later, 0)
 
     for o in wa_offsets:
         f2_copy(o).wait()
@@ -186,15 +186,21 @@
     proj[...] = jnp.zeros_like(proj)
 
     def project(h):
-        def add(c, carry):
-            for o in wa_offsets:
-                mix_copy(c, h, o).wait()
-            hi, lo = split(got[c, h].reshape(depth, LANES))
+        def add(c):
+            hi, lo = split(got[h, :, c].reshape(depth, LANES))
             both = dot(a2[c], hi)
             proj[h] += both[:kept] + both[kept:] + dot(a2[c, :kept, :], lo)
+
+        step = 1 if h == 0 else 2
+
+        def group(g, carry):
+            for o in wa_offsets:
+                mix_copy(g * step, h, o).wait()
+            for n in range(step):
+                add(g * step + n)
             return carry
 
-        lax.fori_loop(0, chunks, add, 0)
+        lax.fori_loop(0, chunks // step, group, 0)
 
     def row_copy(h, o):
         peer = an_peer(o)
@@ -296,8 +302,8 @@
             pltpu.VMEM((per, rank_four, slab, first), F32),
             pltpu.VMEM((nw, fibre, rank_two), F32),
             pltpu.VMEM((chunks, 2 * kept, depth), BF16),
-            pltpu.VMEM((chunks, halves, nw, per, SUB, LANES), F32),
-            pltpu.VMEM((chunks, halves, nw, per, SUB, LANES), F32),
+            pltpu.VMEM((halves, nw, chunks, per, SUB, LANES), F32),
+            pltpu.VMEM((halves, nw, chunks, per, SUB, LANES), F32),
             pltpu.VMEM((halves, kept, LANES), F32),
             pltpu.VMEM((halves, na, share, LANES), F32),
             pltpu.VMEM((na, slab, LANES), F32),

time: 49.2 us -> 50.4 us (1.024)
  Pallas kernels: 47.6 us -> 48.9 us
    pallas_call x1, Pallas kernels: 47.6 us -> 48.9 us  [on_device(): pl.pallas_call(functools.partial(kernel, nw, na, chunks), out_shape=jax.S...]
where the time goes in v4:
time: 50.4 us; the launch traced here: 50.2 us
  Pallas kernels  48.9 us (97%)
  other arithmetic  1.3 us (3%)
    pallas_call x1, Pallas kernels, on_device(): pl.pallas_call(functools.partial(kernel, nw, na, chunks), out_shape=jax.S...  48.9 us
    div x1, other arithmetic, on_device(): return summed[:, :na * slab] / (rank_one * rank_two * rank_four)  1.3 us

profile of v4, /device:TPU:0, one launch (start us, length us, event | category | flops | bytes accessed | tf_op | source)
XLA Modules:
  0.0 50.2 jit_solution(8611174319385373219)
XLA Ops:
  0.0 48.9 %shard_map.46 = f32[16,128]{1,0:T(8,128)} custom-call(f32[64,16,16,256]{3,2,1,0:T(8,128)} %x_hbm.1, f32[64,256]{1,0:T(8,128)} %bitcast.2, f32[16,64]{1,0:T(8,128)} %f2_hbm.1, f32[16,64]{1,0:T(8,128)} %bitcast.3), custom_call_target="tpu_custom_call" | custom-call | tf_op jit(solution)/shard_map/pallas_call | solution.py:289
  48.9 1.3 %slice_multiply_fusion = f32[16,64]{1,0:T(8,128)} fusion(f32[16,128]{1,0:T(8,128)} %shard_map.46), kind=kLoop, calls=%fused_computation | loop fusion | flops 1024 | bytes 8192 | tf_op jit(solution)/shard_map/div | solution.py:324

commit v5 on v2

--- a/solution.py
+++ b/solution.py
@@ -272,7 +272,7 @@
     nw, na = lax.axis_size("wa"), lax.axis_size("an")
     species, fibre, slab, first = mass_field.shape
     rank_one, rank_two, rank_four = factor_one.shape[1], factor_two.shape[1], factor_four.shape[1]
-    chunks = 4
+    chunks = 8
     per = fibre // chunks
     halves = rank_one * rank_four * slab // (nw * SUB * LANES)
     kept = rank_two * SUB

time: 49.2 us -> 49.5 us (level)
  no operation moved by 1% of the time
where the time goes in v5:
time: 49.5 us; the launch traced here: 49.2 us
  Pallas kernels  47.9 us (97%)
  other arithmetic  1.3 us (3%)
    pallas_call x1, Pallas kernels, on_device(): pl.pallas_call(functools.partial(kernel, nw, na, chunks), out_shape=jax.S...  47.9 us
    div x1, other arithmetic, on_device(): return summed[:, :na * slab] / (rank_one * rank_two * rank_four)  1.3 us

profile of v5, /device:TPU:0, one launch (start us, length us, event | category | flops | bytes accessed | tf_op | source)
XLA Modules:
  0.0 49.2 jit_solution(16875913103963630469)
XLA Ops:
  0.0 47.9 %shard_map.46 = f32[16,128]{1,0:T(8,128)} custom-call(f32[64,16,16,256]{3,2,1,0:T(8,128)} %x_hbm.1, f32[64,256]{1,0:T(8,128)} %bitcast.2, f32[16,64]{1,0:T(8,128)} %f2_hbm.1, f32[16,64]{1,0:T(8,128)} %bitcast.3), custom_call_target="tpu_custom_call" | custom-call | tf_op jit(solution)/shard_map/pallas_call | solution.py:283
  47.9 1.3 %slice_multiply_fusion = f32[16,64]{1,0:T(8,128)} fusion(f32[16,128]{1,0:T(8,128)} %shard_map.46), kind=kLoop, calls=%fused_computation | loop fusion | flops 1024 | bytes 8192 | tf_op jit(solution)/shard_map/div | solution.py:318

commit v6 on v2

--- a/solution.py
+++ b/solution.py
@@ -105,17 +105,12 @@
     f1s[rank_one:, :] = f1lo
     f2all[me] = f2_ref[...]
 
-    pl.semaphore_wait(barrier, nw + na - 2)
-
     def f2_copy(o):
         return pltpu.make_async_remote_copy(
             src_ref=f2all.at[me], dst_ref=f2all.at[me],
             send_sem=f2_send.at[o], recv_sem=f2_recv.at[o],
             device_id=(wa_peer(o), mine), device_id_type=MESH,
         )
-
-    for o in wa_offsets:
-        f2_copy(o).start()
 
     def mix_copy(c, h, o):
         peer = wa_peer(o)
@@ -141,13 +136,16 @@
                 lane = qg * width + h * LANES
                 mix[c, h, d, jj] = mixed[rg * SUB : (rg + 1) * SUB, lane : lane + LANES]
 
-    def produce(c, carry):
+    def compute(c):
         for jj in range(per):
             load(c * per + jj).wait()
             one_fibre(c * per + jj, c, jj)
-        send(c, 0)
         for h in range(halves):
             got[c, h, me] = mix[c, h, me]
+
+    def produce(c, carry):
+        compute(c)
+        send(c, 0)
         return carry
 
     def send(c, h):
@@ -159,7 +157,12 @@
             send(c, h)
         return carry
 
-    lax.fori_loop(0, chunks, produce, 0)
+    compute(0)
+    pl.semaphore_wait(barrier, nw + na - 2)
+    send(0, 0)
+    for o in wa_offsets:
+        f2_copy(o).start()
+    lax.fori_loop(1, chunks, produce, 0)
     if halves > 1:
         lax.fori_loop(0, chunks, send_later, 0)
 
@@ -226,12 +229,14 @@
             total = jnp.where(lane_block == b, wide, total)
         return total
 
-    total = None
     for h in range(halves):
         project(h)
         for o in an_offsets:
             row_copy(h, o).start()
         rows[h, mine] = proj[h, pl.ds(pl.multiple_of(mine * share, SUB), share), :]
+
+    total = None
+    for h in range(halves):
         for o in an_offsets:
             row_copy(h, o).wait()
         gram_half = gram_of(h)

time: 49.2 us -> 48.8 us (level)
  no operation moved by 1% of the time
where the time goes in v6:
time: 48.8 us; the launch traced here: 48.6 us
  Pallas kernels  47.3 us (97%)
  other arithmetic  1.3 us (3%)
    pallas_call x1, Pallas kernels, on_device(): pl.pallas_call(functools.partial(kernel, nw, na, chunks), out_shape=jax.S...  47.3 us
    div x1, other arithmetic, on_device(): return summed[:, :na * slab] / (rank_one * rank_two * rank_four)  1.3 us

profile of v6, /device:TPU:0, one launch (start us, length us, event | category | flops | bytes accessed | tf_op | source)
XLA Modules:
  0.0 48.6 jit_solution(11799974046878026568)
XLA Ops:
  0.0 47.3 %shard_map.46 = f32[16,128]{1,0:T(8,128)} custom-call(f32[64,16,16,256]{3,2,1,0:T(8,128)} %x_hbm.1, f32[64,256]{1,0:T(8,128)} %bitcast.2, f32[16,64]{1,0:T(8,128)} %f2_hbm.1, f32[16,64]{1,0:T(8,128)} %bitcast.3), custom_call_target="tpu_custom_call" | custom-call | tf_op jit(solution)/shard_map/pallas_call | solution.py:288
  47.3 1.3 %slice_multiply_fusion = f32[16,64]{1,0:T(8,128)} fusion(f32[16,128]{1,0:T(8,128)} %shard_map.46), kind=kLoop, calls=%fused_computation | loop fusion | flops 1024 | bytes 8192 | tf_op jit(solution)/shard_map/div | solution.py:323

commit v7 on v6

--- a/solution.py
+++ b/solution.py
@@ -97,12 +97,12 @@
     spread = one_hot((n1, rank_four), lambda r: r >> 3, lambda c: c)
     widen = one_hot((species, species * SUB), lambda r: r, lambda c: c >> 3)
     same = (iota((n1, species * SUB), 0) & 7) == (iota((n1, species * SUB), 1) & 7)
-    for half, part4 in enumerate((f4hi, f4lo)):
+    deep = species * SUB
+    for half, part4 in enumerate((f4hi, f4hi, f4lo)):
         full = dot(dot(spread, part4).astype(BF16), widen)
-        a1[half * n1 : (half + 1) * n1, :] = jnp.where(same, full, 0.0).astype(BF16)
+        a1[:, half * deep : (half + 1) * deep] = jnp.where(same, full, 0.0).astype(BF16)
     f1hi, f1lo = split(f1t_ref[...])
-    f1s[:rank_one, :] = f1hi
-    f1s[rank_one:, :] = f1lo
+    f1s[...] = jnp.concatenate([f1hi, f1hi, f1lo], axis=1)
     f2all[me] = f2_ref[...]
 
     def f2_copy(o):
@@ -124,12 +124,10 @@
         for kh in range(slab // SUB):
             block = xbuf[j, :, kh * SUB : (kh + 1) * SUB, :].reshape(species * SUB, first)
             hi, lo = split(block)
-            both = dot(a1[...], hi)
-            reduced = both[:n1] + both[n1:] + dot(a1[:n1, :], lo)
+            reduced = dot(a1[...], jnp.concatenate([hi, lo, hi], axis=0))
             red[jj, :, kh * SUB : (kh + 1) * SUB, :] = reduced.reshape(rank_four, SUB, first)
         hi, lo = split(red[jj].reshape(rank_four * slab, first))
-        both = dot_nt(f1s[...], hi)
-        mixed = both[:rank_one] + both[rank_one:] + dot_nt(f1s[:rank_one, :], lo)
+        mixed = dot_nt(f1s[...], jnp.concatenate([hi, lo, hi], axis=1))
         for d in range(nw):
             rg, qg = d // q_groups, d % q_groups
             for h in range(halves):
@@ -296,8 +294,8 @@
             pltpu.VMEM((rank_four, species), F32),
             dma((3,)),
             pltpu.VMEM((fibre, species, slab, first), F32),
-            pltpu.VMEM((2 * rank_four * SUB, species * SUB), BF16),
-            pltpu.VMEM((2 * rank_one, first), BF16),
+            pltpu.VMEM((rank_four * SUB, 3 * species * SUB), BF16),
+            pltpu.VMEM((rank_one, 3 * first), BF16),
             pltpu.VMEM((per, rank_four, slab, first), F32),
             pltpu.VMEM((nw, fibre, rank_two), F32),
             pltpu.VMEM((chunks, 2 * kept, depth), BF16),

time: 48.8 us -> 49.1 us (level)
  no operation moved by 1% of the time
where the time goes in v7:
time: 49.1 us; the launch traced here: 48.8 us
  Pallas kernels  47.5 us (97%)
  other arithmetic  1.3 us (3%)
    pallas_call x1, Pallas kernels, on_device(): pl.pallas_call(functools.partial(kernel, nw, na, chunks), out_shape=jax.S...  47.5 us
    div x1, other arithmetic, on_device(): return summed[:, :na * slab] / (rank_one * rank_two * rank_four)  1.3 us

profile of v7, /device:TPU:0, one launch (start us, length us, event | category | flops | bytes accessed | tf_op | source)
XLA Modules:
  0.0 48.8 jit_solution(9485936032307721173)
XLA Ops:
  0.0 47.5 %shard_map.46 = f32[16,128]{1,0:T(8,128)} custom-call(f32[64,16,16,256]{3,2,1,0:T(8,128)} %x_hbm.1, f32[64,256]{1,0:T(8,128)} %bitcast.2, f32[16,64]{1,0:T(8,128)} %f2_hbm.1, f32[16,64]{1,0:T(8,128)} %bitcast.3), custom_call_target="tpu_custom_call" | custom-call | tf_op jit(solution)/shard_map/pallas_call | solution.py:286
  47.5 1.3 %slice_multiply_fusion = f32[16,64]{1,0:T(8,128)} fusion(f32[16,128]{1,0:T(8,128)} %shard_map.46), kind=kLoop, calls=%fused_computation | loop fusion | flops 1024 | bytes 8192 | tf_op jit(solution)/shard_map/div | solution.py:321
